TPU v7x, 128 devices: a whole 4x4x4 slice. The times are simulated.
128 devices in a mesh: ctx: 32 (over z, y, core), tp: 4 (over x).
Axes of the slice: x: 4, y: 4, z: 4, core: 2. Of those that a mesh axis runs over, the one named last changes fastest.
Arguments:
- x_tokens: bfloat16 [16384, 4096], P('ctx', 'tp'), may hold values from -60 to 60
- w_query: bfloat16 [4096, 4096], P(None, 'tp'), may hold values from -0.09375 to 0.09375
- w_key: bfloat16 [4096, 1024], P(None, 'tp'), may hold values from -0.09375 to 0.09375
- w_value: bfloat16 [4096, 1024], P(None, 'tp'), may hold values from -0.09375 to 0.09375
- w_output: bfloat16 [4096, 4096], P('tp'), may hold values from -0.09375 to 0.09375
- pattern: int32 [128, 8], P('ctx'), may hold values from 0 to 127, as said below
- doc_lengths: int32 [16], replicated, may hold values from 1 to 10240, 16384 in all
Outputs:
- attn_out: bfloat16 [16384, 4096], P(('ctx', 'tp'))
Inputs may be any that keep to these rules, and one draw needn't show every extreme that they name: `pattern`: row q has 8 entries; the first is q itself and every entry is at most q; entries may repeat. The rows of one index of ctx (4 rows) name at most 2 distinct blocks held by any other index of ctx (index i holding blocks i * 4 onward), and exactly 2 of index 0 for every other index. Every row of an index i in the upper half of ctx names 2 blocks of index i minus half the number of ctx indices.
All inputs are finite; a program needn't handle non-finite values.
Results may differ from a plain program's by a relative error of at most 0.02.
Values may be sent and summed in bfloat16 or wider, within the bound.
No kernel may reach another device: no remote copies, remote signals or barrier semaphores. Data moves between devices by JAX's collectives and lax.ppermute only.
A program may use at most 128 MiB of HBM per device.

v0:
```python
import jax
import jax.numpy as jnp
from jax import lax
from jax.sharding import PartitionSpec as P

HD = 128
BLK = 128
LIST = 8
ROPE_BASE = 500000.0
NEG_LARGE = -1e30


def rotate(projected, head_count, positions):
    split_heads = projected.reshape(projected.shape[0], head_count, HD)
    frequency = ROPE_BASE ** (-(jnp.arange(HD // 2, dtype=jnp.float32) * 2.0 / HD))
    angles = positions.astype(jnp.float32)[:, None] * frequency[None, :]
    cosine_table = jnp.cos(angles)[:, None, :]
    sine_table = jnp.sin(angles)[:, None, :]
    front_half = split_heads[..., : HD // 2]
    back_half = split_heads[..., HD // 2 :]
    return jnp.concatenate(
        [
            front_half * cosine_table - back_half * sine_table,
            back_half * cosine_table + front_half * sine_table,
        ],
        axis=-1,
    )


def document_of(positions, doc_lengths):
    ends = jnp.cumsum(doc_lengths)
    return jnp.sum((ends[None, :] <= positions[:, None]).astype(jnp.int32), axis=1)


def fresh_entries(pattern):
    equal = pattern[:, :, None] == pattern[:, None, :]
    earlier = jnp.tril(jnp.ones((LIST, LIST), dtype=bool), -1)
    return jnp.logical_not(jnp.any(equal & earlier[None], axis=2))


def attend_listed(
    query,
    chosen_keys,
    chosen_values,
    pattern,
    positions,
    documents,
    doc_lengths,
    kv_heads,
    group_size,
):
    local_rows = positions.shape[0]
    block_count = local_rows // BLK
    fresh = fresh_entries(pattern)
    offsets_in = jnp.arange(BLK, dtype=jnp.int32)
    key_index = (pattern[:, :, None] * BLK + offsets_in[None, None, :]).reshape(
        block_count, LIST * BLK
    )
    key_ok = jnp.repeat(fresh, BLK, axis=1)
    key_doc = document_of(key_index.reshape(-1), doc_lengths).reshape(key_index.shape)
    block_pos = positions.reshape(block_count, BLK)
    block_doc = documents.reshape(block_count, BLK)
    block_query = query.reshape(block_count, BLK, kv_heads, group_size, HD)
    allowed = (
        (key_index[:, None, :] <= block_pos[:, :, None])
        & (key_doc[:, None, :] == block_doc[:, :, None])
        & key_ok[:, None, :]
    )
    allowed = allowed[:, None, None, :, :]
    scores = jnp.einsum(
        "bqkgd,blkd->bkgql", block_query, chosen_keys, preferred_element_type=jnp.float32
    )
    masked = jnp.where(allowed, scores, NEG_LARGE)
    row_max = jnp.max(masked, axis=-1, keepdims=True)
    weights = jnp.where(allowed, jnp.exp(masked - row_max), 0.0)
    total = jnp.sum(weights, axis=-1)
    mixed = jnp.einsum(
        "bkgql,blkd->bkgqd",
        weights.astype(jnp.bfloat16),
        chosen_values,
        preferred_element_type=jnp.float32,
    )
    mixed = mixed / total[..., None]
    return (
        jnp.transpose(mixed, (0, 3, 1, 2, 4))
        .reshape(local_rows, kv_heads * group_size * HD)
        .astype(jnp.bfloat16)
    )


def on_device(x_tokens, w_query, w_key, w_value, w_output, pattern, doc_lengths):
    features = lax.all_gather(x_tokens, "tp", axis=1, tiled=True)
    local_rows = features.shape[0]
    query_heads = w_query.shape[1] // HD
    kv_heads = w_key.shape[1] // HD
    group_size = query_heads // kv_heads
    block_count = local_rows // BLK
    positions = lax.axis_index("ctx") * local_rows + jnp.arange(local_rows, dtype=jnp.int32)
    query = rotate(
        jnp.dot(features, w_query, preferred_element_type=jnp.float32), query_heads, positions
    ) * HD ** (-0.5)
    query = query.astype(jnp.bfloat16).reshape(local_rows, kv_heads, group_size, HD)
    keys = rotate(jnp.dot(features, w_key, preferred_element_type=jnp.float32), kv_heads, positions)
    keys = keys.astype(jnp.bfloat16).reshape(local_rows, kv_heads * HD)
    values = jnp.dot(features, w_value, preferred_element_type=jnp.float32).astype(jnp.bfloat16)
    documents = document_of(positions, doc_lengths)
    every_key, every_value = (
        lax.all_gather(keys, "ctx", axis=0, tiled=True),
        lax.all_gather(values, "ctx", axis=0, tiled=True),
    )
    offsets_in = jnp.arange(BLK, dtype=jnp.int32)
    key_index = (pattern[:, :, None] * BLK + offsets_in[None, None, :]).reshape(
        block_count, LIST * BLK
    )
    chosen_keys = every_key[key_index].reshape(block_count, LIST * BLK, kv_heads, HD)
    chosen_values = every_value[key_index].reshape(block_count, LIST * BLK, kv_heads, HD)
    attended = attend_listed(
        query,
        chosen_keys,
        chosen_values,
        pattern,
        positions,
        documents,
        doc_lengths,
        kv_heads,
        group_size,
    )
    return lax.psum_scatter(
        jnp.dot(attended, w_output, preferred_element_type=jnp.float32).astype(jnp.bfloat16),
        "tp",
        scatter_dimension=0,
        tiled=True,
    )


def solution(mesh):
    return jax.shard_map(
        on_device,
        mesh=mesh,
        in_specs=(
            P("ctx", "tp"),
            P(None, "tp"),
            P(None, "tp"),
            P(None, "tp"),
            P("tp", None),
            P("ctx", None),
            P(),
        ),
        out_specs=P(("ctx", "tp"), None),
        check_vma=False,
    )
```

profile of v0, /device:TPU:1, one launch (start us, length us, event | category | flops | bytes accessed | tf_op | source)
XLA Modules:
  0.0 297.7 jit_solution(13942825732113829720)
XLA Ops:
  6.5 0.0 copy-start
  6.5 0.0 all-gather.4.cloned.1.call-start
  6.5 0.7 all-gather.4.cloned.1.call-update
  7.3 0.0 all-gather.8.cloned.1.call-start
  7.3 53.2 %all-gather.4.cloned.1.call-done = bf16[512,4096]{1,0:T(8,128)(2,1)} async-done(((bf16[512,1024]{1,0:T(8,128)(2,1)}), bf16[512,4096]{1,0:T(8,128)(2,1)}) %all-gather.4.cloned.1.call-update) | async-done | bytes 4194320 | tf_op jit(solution)/shard_map/all_gather | solution.py:92
  60.5 0.0 copy-done
  60.5 4.1 %convolution_convert_fusion.1 = bf16[512,256]{1,0:T(8,128)(2,1)} fusion(bf16[512,4096]{1,0:T(8,128)(2,1)} %all-gather.4.cloned.1.call-done, bf16[4096,256]{1,0:T(8,128)(2,1)S(1)} %copy-done), kind=kOutput, calls=%fused_computation.19 | convolution fusion | flops 1073872896 | bytes 6553600 | tf_op jit(solution)/shard_map/dot_general | solution.py:105
  64.6 0.0 all-gather.8.cloned.1.call-update
  64.6 0.0 all-gather.6.cloned.1.call-start
  64.7 0.5 multiply_cosine_fusion
  65.2 4.2 %fusion.23 = f32[512,256]{0,1:T(8,128)S(1)} fusion(bf16[512,4096]{1,0:T(8,128)(2,1)} %all-gather.4.cloned.1.call-done, bf16[4096,256]{1,0:T(8,128)(2,1)} %param.9), kind=kOutput, calls=%fused_computation.51 | convolution fusion | flops 1073741824 | bytes 6815744 | tf_op jit(solution)/shard_map/dot_general | solution.py:103
  69.4 0.0 copy-start.4
  69.4 0.0 copy-start.5
  69.4 0.1 subtract_convert_fusion
  69.6 0.9 copy.38
  70.4 0.0 all-gather.6.cloned.1.call-update
  70.4 0.2 reduce-scatter.2.cloned.1.call-start
  70.7 0.1 iota_compare_fusion
  70.8 0.0 copy-done.4
  70.8 0.2 and_reduce_fusion
  71.0 0.1 broadcast_bitcast_fusion.1
  71.1 0.1 copy.25
  71.2 0.1 reduce
  71.3 0.1 add.112
  71.4 0.1 broadcast_bitcast_fusion
  71.5 0.1 convert_reduce_fusion
  71.7 0.1 convert_reduce_fusion.1
  71.8 3.9 %and_and_fusion = pred[4,128,1024]{1,2,0:T(8,128)(4,1)} fusion(s32[4,128]{1,0:T(4,128)S(1)} %bitcast.60, s32[4,1024]{1,0:T(4,128)S(1)} %eq.34, s32[4,128]{1,0:T(4,128)S(1)} %add_add_fusion, s32[4,1024]{1,0:T(4,128)S(1)} %bitcast_add_fusion, pred[4,1024]{1,0:T(4,128)(4,1)S(1)} %bitcast.59), kind=kLoop, calls=%fused_computation.18 | loop fusion | flops 2097152 | bytes 565248 | tf_op jit(solution)/shard_map/and | solution.py:65
  75.7 8.3 %fusion.24 = f32[512,1024]{0,1:T(8,128)S(1)} fusion(bf16[512,4096]{1,0:T(8,128)(2,1)} %all-gather.4.cloned.1.call-done, bf16[4096,1024]{1,0:T(8,128)(2,1)} %param.8), kind=kOutput, calls=%fused_computation.52 | convolution fusion | flops 4294967296 | bytes 14680064 | tf_op jit(solution)/shard_map/reshape | solution.py:14
  84.0 0.3 multiply_subtract_fusion
  84.3 1.3 concatenate.13
  85.6 1.7 copy.29
  87.4 1.3 concatenate.14
  88.7 2.7 copy.30
  91.4 27.2 %all-gather.8.cloned.1.call-done = bf16[16384,256]{1,0:T(8,128)(2,1)} async-done(((bf16[512,256]{1,0:T(8,128)(2,1)}), bf16[16384,256]{1,0:T(8,128)(2,1)}) %all-gather.8.cloned.1.call-update) | async-done | bytes 8388624 | tf_op jit(solution)/shard_map/all_gather | solution.py:109
  118.6 20.4 %gather_fusion.1 = bf16[4096,256]{1,0:T(8,128)(2,1)} fusion(bf16[16384,256]{1,0:T(8,128)(2,1)} %all-gather.8.cloned.1.call-done, s32[4096]{0:T(1024)S(1)} %bitcast_clamp_fusion), kind=kCustom, calls=%fused_computation.1 | custom fusion | bytes 4210688 | tf_op jit(solution)/shard_map/gather | solution.py:116
  139.0 4.0 %reshape.220 = bf16[4,1024,2,128]{3,2,1,0:T(2,128)(2,1)} reshape(bf16[4096,256]{1,0:T(8,128)(2,1)} %gather_fusion.1) | data formatting | bytes 4194304 | tf_op jit(solution)/shard_map/reshape | solution.py:116
  143.0 30.5 %all-gather.6.cloned.1.call-done = bf16[16384,256]{1,0:T(8,128)(2,1)} async-done(((bf16[512,256]{1,0:T(8,128)(2,1)}), bf16[16384,256]{1,0:T(8,128)(2,1)}) %all-gather.6.cloned.1.call-update) | async-done | bytes 8388624 | tf_op jit(solution)/shard_map/all_gather | solution.py:108
  173.4 20.4 %gather_fusion = bf16[4096,256]{1,0:T(8,128)(2,1)} fusion(bf16[16384,256]{1,0:T(8,128)(2,1)} %all-gather.6.cloned.1.call-done, s32[4096]{0:T(1024)S(1)} %bitcast_clamp_fusion), kind=kCustom, calls=%fused_computation | custom fusion | bytes 4210688 | tf_op jit(solution)/shard_map/gather | solution.py:115
  193.8 4.0 %reshape.218 = bf16[4,1024,2,128]{3,2,1,0:T(2,128)(2,1)} reshape(bf16[4096,256]{1,0:T(8,128)(2,1)} %gather_fusion) | data formatting | bytes 4194304 | tf_op jit(solution)/shard_map/reshape | solution.py:115
  197.8 10.5 %fusion.9 = f32[4,2,1024,128,4]{3,2,4,1,0:T(8,128)} fusion(bf16[4,1024,2,128,1]{3,2,1,0,4:T(2,128)(2,1)} %bitcast.54, f32[4,128,2,4,64]{4,1,3,2,0:T(8,128)} %copy.30, f32[4,128,2,4,64]{4,1,3,2,0:T(8,128)S(1)} %copy.29), kind=kOutput, calls=%fused_computation.16 | convolution fusion | flops 1075314688 | bytes 20971520 | tf_op jit(solution)/shard_map/bqkgd,blkd->bkgql/dot_general | solution.py:70
  208.3 19.6 %fusion.22 = (f32[4,2,4,128]{3,2,1,0:T(4,128)S(1)}, bf16[4,2,4,128,1024]{3,4,2,1,0:T(8,128)(2,1)}) fusion(f32[4,2,1024,128,4]{3,2,4,1,0:T(8,128)} %fusion.9, pred[4,128,1024]{1,2,0:T(8,128)(4,1)S(1)} %copy-done.3), kind=kOutput, calls=%fused_computation.50 | output fusion | flops 25166848 | bytes 25706496 | tf_op jit(solution)/shard_map/sub | solution.py:75
  227.9 6.2 %fusion.7 = bf16[4,128,2,4,128]{4,1,3,2,0:T(8,128)(2,1)S(1)} fusion(f32[4,128,2,4]{1,3,2,0:T(4,128)S(1)} %bitcast.62, bf16[4,1024,2,128,1]{3,2,1,0,4:T(2,128)(2,1)S(1)} %bitcast.55, bf16[4,2,4,128,1024]{3,4,2,1,0:T(8,128)(2,1)} %get-tuple-element.14), kind=kOutput, calls=%fused_computation.14 | convolution fusion | flops 1074790400 | bytes 11550720 | tf_op jit(solution)/shard_map/bkgql,blkd->bkgqd/dot_general | solution.py:77
  234.1 0.8 copy.34
  234.9 0.8 convert_element_type.46
  235.7 9.4 %convolution_convert_fusion = bf16[512,4096]{1,0:T(8,128)(2,1)} fusion(bf16[512,1024]{1,0:T(8,128)(2,1)S(1)} %convert_element_type.46, bf16[1024,4096]{1,0:T(8,128)(2,1)} %param.11), kind=kOutput, calls=%fused_computation.10 | convolution fusion | flops 4297064448 | bytes 13631488 | tf_op jit(solution)/shard_map/dot_general | solution.py:129
  245.1 0.0 reduce-scatter.2.cloned.1.call-update
  245.1 46.0 %reduce-scatter.2.cloned.1.call-done = bf16[128,4096]{1,0:T(8,128)(2,1)} async-done(((bf16[512,4096]{1,0:T(8,128)(2,1)}), bf16[128,4096]{1,0:T(8,128)(2,1)}) %reduce-scatter.2.cloned.1.call-update) | async-done | bytes 1048592 | tf_op jit(solution)/shard_map/reduce_scatter | solution.py:128
  (22 shorter events, 0.2 us)
Async XLA Ops:
  6.5 53.9 %copy-start = (bf16[4096,256]{1,0:T(8,128)(2,1)S(1)}, bf16[4096,256]{1,0:T(8,128)(2,1)}, u32[]{:S(2)}) copy-start(bf16[4096,256]{1,0:T(8,128)(2,1)} %param.10) | copy-start | bytes 6291460
  6.5 53.9 %all-gather.4.cloned.1.call-start = ((), (), s32[]{:S(2)}) async-start(), calls=%async_computation.1 | async-start | bytes 5242880 | tf_op jit(solution)/shard_map/all_gather | solution.py:92
  7.3 111.4 %all-gather.8.cloned.1.call-start = ((), (), s32[]{:S(2)}) async-start(), calls=%async_computation.3 | async-start | bytes 8650752 | tf_op jit(solution)/shard_map/all_gather | solution.py:109
  64.6 108.8 %all-gather.6.cloned.1.call-start = ((), (), s32[]{:S(2)}) async-start(), calls=%async_computation.2 | async-start | bytes 8650752 | tf_op jit(solution)/shard_map/all_gather | solution.py:108
  69.4 1.4 copy-start.4
  69.4 1.7 copy-start.5
  70.4 220.7 %reduce-scatter.2.cloned.1.call-start = ((), (), s32[]{:S(2)}) async-start(), calls=%async_computation.4 | async-start | bytes 5242880 | tf_op jit(solution)/shard_map/reduce_scatter | solution.py:128
  197.8 10.5 %copy-start.3 = (pred[4,128,1024]{1,2,0:T(8,128)(4,1)S(1)}, pred[4,128,1024]{1,2,0:T(8,128)(4,1)}, u32[]{:S(2)}) copy-start(pred[4,128,1024]{1,2,0:T(8,128)(4,1)} %and_and_fusion) | copy-start | bytes 1572868
  208.3 19.6 %copy-start.2 = (bf16[4,1024,2,128]{3,2,1,0:T(2,128)(2,1)S(1)}, bf16[4,1024,2,128]{3,2,1,0:T(2,128)(2,1)}, u32[]{:S(2)}) copy-start(bf16[4,1024,2,128]{3,2,1,0:T(2,128)(2,1)} %reshape.220) | copy-start | bytes 6291460
  245.1 46.1 %copy-start.1 = (bf16[4096,256]{1,0:T(8,128)(2,1)S(1)}, bf16[4096,256]{1,0:T(8,128)(2,1)}, u32[]{:S(2)}) copy-start(bf16[4096,256]{1,0:T(8,128)(2,1)} %param.10) | copy-start | bytes 6291460
Sparse Core Ops, SparseCore 0:
  9.0 51.3 all-gather.3
  64.7 53.8 all-gather.7
  120.9 52.5 all-gather.5
  245.2 45.8 reduce-scatter.1
where the time goes:
time: 298 us
  waiting for transfers between devices  158 us (53%)
  local copies, waits for them, and re-layouts  58.6 us (20%)
  matrix products  42.6 us (14%)
  other arithmetic  25.3 us (8%)
  between operations  13.3 us (4%)
    all_gather x1, waiting for transfers between devices, on_device(): features = lax.all_gather(x_tokens, 'tp', axis=1, tiled=True)  53.2 us
    reduce_scatter x1, waiting for transfers between devices, on_device(): lax.psum_scatter(jnp.dot(attended, w_output, preferred_element_type=jnp.f...  46 us
    all_gather x1, waiting for transfers between devices, on_device(): lax.all_gather(keys, 'ctx', axis=0, tiled=True)  30.5 us
    all_gather x1, waiting for transfers between devices, on_device(): lax.all_gather(values, 'ctx', axis=0, tiled=True)  27.2 us
    gather x1, local copies, waits for them, and re-layouts, on_device(): every_key[key_index].reshape(block_count, LIST * BLK, kv_heads, HD)  20.4 us
    gather x1, local copies, waits for them, and re-layouts, on_device(): every_value[key_index].reshape(block_count, LIST * BLK, kv_heads, HD)  20.4 us
    sub x1, other arithmetic, attend_listed(): weights = jnp.where(allowed, jnp.exp(masked - row_max), 0.0)  19.6 us
    dot_general x1, matrix products, attend_listed(): jnp.einsum('bqkgd,blkd->bkgql', block_query, chosen_keys, preferred_eleme...  10.5 us
  transfers between devices with their start and end apart: 4, of which 4 were waited for; matrix products, arithmetic and copies ran while one was open for 17% of the time, Pallas kernels for 0%

commit v1 on v0

--- a/solution.py
+++ b/solution.py
@@ -8,6 +8,18 @@
 LIST = 8
 ROPE_BASE = 500000.0
 NEG_LARGE = -1e30
+
+
+def collect(array, axis, dim):
+    ways, here, step = (lax.axis_size(axis), lax.axis_index(axis), array.shape[dim])
+    line, have = (array, 1)
+    while have < ways:
+        line = jnp.concatenate(
+            [line, lax.ppermute(line, axis, [(d, (d - have) % ways) for d in range(ways)])],
+            axis=dim,
+        )
+        have = 2 * have
+    return jnp.roll(line, here * step, axis=dim)
 
 
 def rotate(projected, head_count, positions):
@@ -106,7 +118,7 @@
     documents = document_of(positions, doc_lengths)
     every_key, every_value = (
         lax.all_gather(keys, "ctx", axis=0, tiled=True),
-        lax.all_gather(values, "ctx", axis=0, tiled=True),
+        collect(values, "ctx", 0),
     )
     offsets_in = jnp.arange(BLK, dtype=jnp.int32)
     key_index = (pattern[:, :, None] * BLK + offsets_in[None, None, :]).reshape(

time: 298 us -> 449 us (1.51)
  waiting for transfers between devices: 158 us -> 268 us
  local copies, waits for them, and re-layouts: 58.6 us -> 83.9 us
  starting transfers between devices: 0.31 us -> 13.6 us
    ppermute x0 -> x5, waiting for transfers between devices: none -> 167 us  [collect(): lax.ppermute(line, axis, [(d, (d - have) % ways) for d in range(ways)])]
    all_gather x1, waiting for transfers between devices: 30.5 us -> 0.01 us  [on_device(): lax.all_gather(keys, 'ctx', axis=0, tiled=True)]
    all_gather x1 -> x0, waiting for transfers between devices: 27.2 us -> none  [on_device(): lax.all_gather(values, 'ctx', axis=0, tiled=True)]
    unnamed x14 -> x33, local copies, waits for them, and re-layouts: 0.11 us -> 14.2 us
    ppermute x0 -> x5, starting transfers between devices: none -> 13.5 us  [collect(): lax.ppermute(line, axis, [(d, (d - have) % ways) for d in range(ways)])]
    dynamic_slice x0 -> x1, local copies, waits for them, and re-layouts: none -> 7.02 us  [collect(): return jnp.roll(line, here * step, axis=dim)]
    concatenate x0 -> x2, local copies, waits for them, and re-layouts: none -> 6.75 us  [the longest x1 4.38 us: collect(): return jnp.roll(line, here * step, axis=dim)]
  transfers between devices with their start and end apart: 4 -> 8, of which waited for: 4 -> 7; matrix products, arithmetic and copies ran while one was open for 17% -> 17% of each run, Pallas kernels for 0% -> 0%
where the time goes in v1:
time: 449 us
  waiting for transfers between devices  268 us (60%)
  local copies, waits for them, and re-layouts  83.9 us (19%)
  matrix products  42.9 us (10%)
  other arithmetic  26.6 us (6%)
  starting transfers between devices  13.6 us (3%)
  between operations  13.3 us (3%)
    ppermute x5, waiting for transfers between devices, collect(): lax.ppermute(line, axis, [(d, (d - have) % ways) for d in range(ways)])  167 us
    all_gather x1, waiting for transfers between devices, on_device(): features = lax.all_gather(x_tokens, 'tp', axis=1, tiled=True)  52.6 us
    reduce_scatter x1, waiting for transfers between devices, on_device(): lax.psum_scatter(jnp.dot(attended, w_output, preferred_element_type=jnp.f...  48.4 us
    gather x1, local copies, waits for them, and re-layouts, on_device(): every_key[key_index].reshape(block_count, LIST * BLK, kv_heads, HD)  20.4 us
    sub x1, other arithmetic, attend_listed(): weights = jnp.where(allowed, jnp.exp(masked - row_max), 0.0)  19.8 us
    gather x1, local copies, waits for them, and re-layouts, on_device(): every_value[key_index].reshape(block_count, LIST * BLK, kv_heads, HD)  17.4 us
    unnamed x33, local copies, waits for them, and re-layouts  14.2 us
    ppermute x5, starting transfers between devices, collect(): lax.ppermute(line, axis, [(d, (d - have) % ways) for d in range(ways)])  13.5 us
  transfers between devices with their start and end apart: 8, of which 7 were waited for; matrix products, arithmetic and copies ran while one was open for 17% of the time, Pallas kernels for 0%

profile of v1, /device:TPU:1, one launch (start us, length us, event | category | flops | bytes accessed | tf_op | source)
XLA Modules:
  0.0 448.6 jit_solution(16691209694195011422)
XLA Ops:
  6.5 0.7 all-gather.3.cloned.1.call-update
  7.3 0.5 multiply_cosine_fusion
  7.9 52.6 %all-gather.3.cloned.1.call-done = bf16[512,4096]{1,0:T(8,128)(2,1)} async-done(((bf16[512,1024]{1,0:T(8,128)(2,1)}), bf16[512,4096]{1,0:T(8,128)(2,1)}) %all-gather.3.cloned.1.call-update) | async-done | bytes 4194320 | tf_op jit(solution)/shard_map/all_gather | solution.py:104
  60.5 4.2 fusion.23
  64.8 0.8 copy.38
  65.7 4.2 constant_dynamic-update-slice_fusion.4
  69.9 0.7 collective-permute-start
  70.6 5.1 %collective-permute-done = bf16[512,256]{1,0:T(8,128)(2,1)S(1)} collective-permute-done((bf16[512,256]{1,0:T(8,128)(2,1)S(1)}, bf16[512,256]{1,0:T(8,128)(2,1)S(1)}, u32[]{:S(2)}, u32[]{:S(2)}) %collective-permute-start) | collective-permute-done | bytes 262176 | tf_op jit(solution)/shard_map/ppermute | solution.py:18
  75.8 9.7 %collective-permute-start.1 = (bf16[1024,256]{1,0:T(8,128)(2,1)S(1)}, bf16[1024,256]{1,0:T(8,128)(2,1)S(1)}, u32[]{:S(2)}, u32[]{:S(2)}) collective-permute-start(bf16[1024,256]{1,0:T(8,128)(2,1)S(1)} %pad_maximum_fusion.2), channel_id=1, source_target_pairs={{0,120},{4,124},{8,0},{12,4},{16,8},{20,12},{24,16},{28,20},{32,24... | collective-permute-start | bytes 1572872 | tf_op jit(solution)/shard_map/ppermute | solution.py:18
  85.5 9.6 %collective-permute-done.1 = bf16[1024,256]{1,0:T(8,128)(2,1)S(1)} collective-permute-done((bf16[1024,256]{1,0:T(8,128)(2,1)S(1)}, bf16[1024,256]{1,0:T(8,128)(2,1)S(1)}, u32[]{:S(2)}, u32[]{:S(2)}) %collective-permute-start.1) | collective-permute-done | bytes 524320 | tf_op jit(solution)/shard_map/ppermute | solution.py:18
  95.2 3.0 collective-permute-start.2
  98.2 38.4 %collective-permute-done.2 = bf16[2048,256]{1,0:T(8,128)(2,1)S(1)} collective-permute-done((bf16[2048,256]{1,0:T(8,128)(2,1)S(1)}, bf16[2048,256]{1,0:T(8,128)(2,1)S(1)}, u32[]{:S(2)}, u32[]{:S(2)}) %collective-permute-start.2) | collective-permute-done | bytes 1048608 | tf_op jit(solution)/shard_map/ppermute | solution.py:18
  136.7 0.1 pad_maximum_fusion
  136.9 0.8 constant_dynamic-update-slice_fusion.3
  137.7 1.1 constant_dynamic-update-slice_fusion.2
  138.8 1.5 constant_dynamic-update-slice_fusion.1
  140.3 43.2 %collective-permute-done.3 = bf16[4096,256]{1,0:T(8,128)(2,1)S(1)} collective-permute-done((bf16[4096,256]{1,0:T(8,128)(2,1)S(1)}, bf16[4096,256]{1,0:T(8,128)(2,1)S(1)}, u32[]{:S(2)}, u32[]{:S(2)}) %collective-permute-start.3) | collective-permute-done | bytes 2097184 | tf_op jit(solution)/shard_map/ppermute | solution.py:18
  183.5 1.4 copy-done.2
  184.9 2.4 constant_dynamic-update-slice_fusion
  187.7 0.1 convert_reduce_fusion
  187.9 0.2 and_reduce_fusion
  188.4 3.9 and_and_fusion
  192.3 8.3 %fusion.24 = f32[512,1024]{0,1:T(8,128)S(1)} fusion(bf16[512,4096]{1,0:T(8,128)(2,1)} %all-gather.3.cloned.1.call-done, bf16[4096,1024]{1,0:T(8,128)(2,1)} %param.8), kind=kOutput, calls=%fused_computation.73 | convolution fusion | flops 4294967296 | bytes 14680064 | tf_op jit(solution)/shard_map/reshape | solution.py:26
  200.6 1.3 multiply_subtract_fusion
  201.8 2.6 concatenate.35
  204.4 2.7 copy.29
  207.1 1.3 concatenate.36
  208.4 2.7 copy.30
  211.1 70.1 %collective-permute-done.4 = bf16[8192,256]{1,0:T(8,128)(2,1)} collective-permute-done((bf16[8192,256]{1,0:T(8,128)(2,1)}, bf16[8192,256]{1,0:T(8,128)(2,1)}, u32[]{:S(2)}, u32[]{:S(2)}) %collective-permute-start.4) | collective-permute-done | bytes 4194336 | tf_op jit(solution)/shard_map/ppermute | solution.py:18
  281.3 4.4 constant_dynamic-update-slice_fusion.11
  285.7 0.7 constant_dynamic-update-slice_fusion.10
  286.5 0.8 constant_dynamic-update-slice_fusion.9
  287.2 0.9 constant_dynamic-update-slice_fusion.8
  288.1 1.0 constant_dynamic-update-slice_fusion.7
  289.1 1.5 constant_dynamic-update-slice_fusion.6
  290.6 4.4 constant_dynamic-update-slice_fusion.5
  294.9 7.0 %constant_dynamic-slice_fusion = bf16[16384,256]{1,0:T(8,128)(2,1)} fusion(bf16[32768,256]{1,0:T(8,128)(2,1)} %constant_dynamic-update-slice_fusion.5, s32[]{:T(128)S(6)} %select_n.37), kind=kLoop, calls=%fused_computation.68 | loop fusion | bytes 16777220 | tf_op jit(solution)/shard_map/jit(_roll_dynamic)/dynamic_slice | solution.py:22
  302.0 17.4 %gather_fusion.1 = bf16[4096,256]{1,0:T(8,128)(2,1)S(1)} fusion(bf16[16384,256]{1,0:T(8,128)(2,1)} %constant_dynamic-slice_fusion, s32[4096]{0:T(1024)S(1)} %bitcast_clamp_fusion), kind=kCustom, calls=%fused_computation.1 | custom fusion | bytes 4210688 | tf_op jit(solution)/shard_map/gather | solution.py:128
  319.4 2.1 reshape.220
  321.6 20.4 %gather_fusion = bf16[4096,256]{1,0:T(8,128)(2,1)} fusion(bf16[16384,256]{1,0:T(8,128)(2,1)} %all-gather.5.cloned.1.call-done, s32[4096]{0:T(1024)S(1)} %bitcast_clamp_fusion), kind=kCustom, calls=%fused_computation | custom fusion | bytes 4210688 | tf_op jit(solution)/shard_map/gather | solution.py:127
  341.9 4.1 reshape.218
  346.1 10.5 %fusion.9 = f32[4,2,1024,128,4]{3,2,4,1,0:T(8,128)} fusion(bf16[4,1024,2,128,1]{3,2,1,0,4:T(2,128)(2,1)} %bitcast.54, f32[4,128,2,4,64]{4,1,3,2,0:T(8,128)} %copy.30, f32[4,128,2,4,64]{4,1,3,2,0:T(8,128)S(1)} %copy-done.4), kind=kOutput, calls=%fused_computation.17 | convolution fusion | flops 1075314688 | bytes 20971520 | tf_op jit(solution)/shard_map/bqkgd,blkd->bkgql/dot_general | solution.py:82
  356.6 19.8 %fusion.22 = (f32[4,2,4,128]{3,2,1,0:T(4,128)S(1)}, bf16[4,2,4,128,1024]{3,4,2,1,0:T(8,128)(2,1)}) fusion(f32[4,2,1024,128,4]{3,2,4,1,0:T(8,128)} %fusion.9, pred[4,128,1024]{1,2,0:T(8,128)(4,1)S(1)} %copy-done.8), kind=kOutput, calls=%fused_computation.71 | output fusion | flops 25166848 | bytes 25706496 | tf_op jit(solution)/shard_map/sub | solution.py:87
  376.3 6.2 %fusion.7 = bf16[4,128,2,4,128]{4,1,3,2,0:T(8,128)(2,1)S(1)} fusion(f32[4,128,2,4]{1,3,2,0:T(4,128)S(1)} %bitcast.62, bf16[4,1024,2,128,1]{3,2,1,0,4:T(2,128)(2,1)S(1)} %bitcast.55, bf16[4,2,4,128,1024]{3,4,2,1,0:T(8,128)(2,1)} %get-tuple-element.24), kind=kOutput, calls=%fused_computation.15 | convolution fusion | flops 1074790400 | bytes 11550720 | tf_op jit(solution)/shard_map/bkgql,blkd->bkgqd/dot_general | solution.py:89
  382.5 0.8 copy.34
  383.4 0.8 convert_element_type.46
  384.1 9.5 %convolution_convert_fusion = bf16[512,4096]{1,0:T(8,128)(2,1)} fusion(bf16[512,1024]{1,0:T(8,128)(2,1)S(1)} %convert_element_type.46, bf16[1024,4096]{1,0:T(8,128)(2,1)} %param.11), kind=kOutput, calls=%fused_computation.10 | convolution fusion | flops 4297064448 | bytes 13631488 | tf_op jit(solution)/shard_map/dot_general | solution.py:141
  393.7 48.4 %reduce-scatter.2.cloned.1.call-done = bf16[128,4096]{1,0:T(8,128)(2,1)} async-done(((bf16[512,4096]{1,0:T(8,128)(2,1)}), bf16[128,4096]{1,0:T(8,128)(2,1)}) %reduce-scatter.2.cloned.1.call-update) | async-done | bytes 1048592 | tf_op jit(solution)/shard_map/reduce_scatter | solution.py:140
  (54 shorter events, 1.2 us)
Async XLA Ops:
  6.5 59.1 %copy-start = (bf16[4096,256]{1,0:T(8,128)(2,1)S(1)}, bf16[4096,256]{1,0:T(8,128)(2,1)}, u32[]{:S(2)}) copy-start(bf16[4096,256]{1,0:T(8,128)(2,1)} %param.10) | copy-start | bytes 6291460
  6.5 53.9 %all-gather.3.cloned.1.call-start = ((), (), s32[]{:S(2)}) async-start(), calls=%async_computation.1 | async-start | bytes 5242880 | tf_op jit(solution)/shard_map/all_gather | solution.py:104
  7.3 314.3 %all-gather.5.cloned.1.call-start = ((), (), s32[]{:S(2)}) async-start(), calls=%async_computation.2 | async-start | bytes 8650752 | tf_op jit(solution)/shard_map/all_gather | solution.py:120
  7.9 56.8 %copy-start.6 = (f32[512,64]{0,1:T(8,128)}, f32[512,64]{0,1:T(8,128)S(1)}, u32[]{:S(2)}) copy-start(f32[512,64]{0,1:T(8,128)S(1)} %get-tuple-element.20) | copy-start | bytes 393220
  65.6 376.5 %reduce-scatter.2.cloned.1.call-start = ((), (), s32[]{:S(2)}) async-start(), calls=%async_computation.3 | async-start | bytes 5242880 | tf_op jit(solution)/shard_map/reduce_scatter | solution.py:140
  69.9 5.9 %collective-permute-start = (bf16[512,256]{1,0:T(8,128)(2,1)S(1)}, bf16[512,256]{1,0:T(8,128)(2,1)S(1)}, u32[]{:S(2)}, u32[]{:S(2)}) collective-permute-start(bf16[512,256]{1,0:T(8,128)(2,1)S(1)} %get-tuple-element.25), channel_id=1, source_target_pairs={{0,124},{4,0},{8,4},{12,8},{16,12},{20,16},{24,20},{28,24},{32,28}... | collective-permute-start | bytes 786440 | tf_op jit(solution)/shard_map/ppermute | solution.py:18
  75.8 19.3 %collective-permute-start.1 = (bf16[1024,256]{1,0:T(8,128)(2,1)S(1)}, bf16[1024,256]{1,0:T(8,128)(2,1)S(1)}, u32[]{:S(2)}, u32[]{:S(2)}) collective-permute-start(bf16[1024,256]{1,0:T(8,128)(2,1)S(1)} %pad_maximum_fusion.2), channel_id=1, source_target_pairs={{0,120},{4,124},{8,0},{12,4},{16,8},{20,12},{24,16},{28,20},{32,24... | collective-permute-start | bytes 1572872 | tf_op jit(solution)/shard_map/ppermute | solution.py:18
  95.2 41.5 %collective-permute-start.2 = (bf16[2048,256]{1,0:T(8,128)(2,1)S(1)}, bf16[2048,256]{1,0:T(8,128)(2,1)S(1)}, u32[]{:S(2)}, u32[]{:S(2)}) collective-permute-start(bf16[2048,256]{1,0:T(8,128)(2,1)S(1)} %pad_maximum_fusion.1), channel_id=1, source_target_pairs={{0,112},{4,116},{8,120},{12,124},{16,0},{20,4},{24,8},{28,12},{32,... | collective-permute-start | bytes 3145736 | tf_op jit(solution)/shard_map/ppermute | solution.py:18
  136.8 46.7 %collective-permute-start.3 = (bf16[4096,256]{1,0:T(8,128)(2,1)S(1)}, bf16[4096,256]{1,0:T(8,128)(2,1)S(1)}, u32[]{:S(2)}, u32[]{:S(2)}) collective-permute-start(bf16[4096,256]{1,0:T(8,128)(2,1)S(1)} %pad_maximum_fusion), channel_id=1, source_target_pairs={{0,96},{4,100},{8,104},{12,108},{16,112},{20,116},{24,120},{28,124... | collective-permute-start | bytes 6291464 | tf_op jit(solution)/shard_map/ppermute | solution.py:18
  138.8 48.4 %copy-start.9 = (s32[4,8]{1,0:T(4,128)S(1)}, s32[4,8]{1,0:T(4,128)}, u32[]{:S(2)}) copy-start(s32[4,8]{1,0:T(4,128)} %param.12) | copy-start | bytes 388
  138.8 48.5 %copy-start.10 = (s32[16]{0:T(128)S(1)}, s32[16]{0:T(128)}, u32[]{:S(2)}) copy-start(s32[16]{0:T(128)} %param.13) | copy-start | bytes 196
  183.5 1.4 copy-start.2
  187.2 94.0 %collective-permute-start.4 = (bf16[8192,256]{1,0:T(8,128)(2,1)}, bf16[8192,256]{1,0:T(8,128)(2,1)}, u32[]{:S(2)}, u32[]{:S(2)}) collective-permute-start(bf16[8192,256]{1,0:T(8,128)(2,1)} %get-tuple-element.7), channel_id=1, source_target_pairs={{0,64},{4,68},{8,72},{12,76},{16,80},{20,84},{24,88},{28,92},{32,9... | collective-permute-start | bytes 12582920 | tf_op jit(solution)/shard_map/ppermute | solution.py:18
  192.3 8.3 %copy-start.7 = (f32[512,64]{0,1:T(8,128)S(1)}, f32[512,64]{0,1:T(8,128)}, u32[]{:S(2)}) copy-start(f32[512,64]{0,1:T(8,128)} %copy-done.6) | copy-start | bytes 393220
  285.7 3.4 copy-start.3
  341.9 4.1 copy-start.4
  346.1 10.5 %copy-start.8 = (pred[4,128,1024]{1,2,0:T(8,128)(4,1)S(1)}, pred[4,128,1024]{1,2,0:T(8,128)(4,1)}, u32[]{:S(2)}) copy-start(pred[4,128,1024]{1,2,0:T(8,128)(4,1)} %and_and_fusion) | copy-start | bytes 1572868
  356.6 19.8 %copy-start.5 = (bf16[4,1024,2,128]{3,2,1,0:T(2,128)(2,1)S(1)}, bf16[4,1024,2,128]{3,2,1,0:T(2,128)(2,1)}, u32[]{:S(2)}) copy-start(bf16[4,1024,2,128]{3,2,1,0:T(2,128)(2,1)} %reshape.220) | copy-start | bytes 6291460
  384.1 58.0 %copy-start.1 = (bf16[4096,256]{1,0:T(8,128)(2,1)S(1)}, bf16[4096,256]{1,0:T(8,128)(2,1)}, u32[]{:S(2)}) copy-start(bf16[4096,256]{1,0:T(8,128)(2,1)} %param.10) | copy-start | bytes 6291460
Sparse Core Ops, SparseCore 0:
  9.0 51.3 all-gather.2
  65.8 75.1 all-gather.4
  393.8 48.2 reduce-scatter.1
